TPU v7x, 256 devices: a whole 4x4x8 slice. The times are simulated.
256 devices in a mesh: lat: 32 (over x, y, core), lev: 8 (over z).
Axes of the slice: x: 4, y: 4, z: 8, core: 2. Of those that a mesh axis runs over, the one named last changes fastest.
Arguments:
- grid_field: bfloat16 [1280, 64, 2560], P('lat', 'lev'), may hold values from -6 to 6
- lon_count: int32 [1280], P('lat'), may hold values from 20 to 2560, as said below
- wave_table: int32 [1280], replicated, may hold values from 0 to 1279, as said below
- legendre: bfloat16 [1280, 640, 1280], P(('lat', 'lev')), may hold values from -0.25 to 0.25
- vertical: float32 [64, 64], replicated, may hold values from -0.8 to 2.5, as said below
Outputs:
- spectral: float32 [64, 2, 1280, 1280], P(None, None, ('lat', 'lev'))
Inputs may be any that keep to these rules, and one draw needn't show every extreme that they name: `lon_count`: multiples of 4, 2560 at the two latitudes next to the equator, 20 at the poles. `wave_table`: A permutation of the wavenumbers: slot r of group g holds r * 256 + p(g) for even r and r * 256 + 255 - p(g) for odd r, for one permutation p of the groups. `vertical`: zero where the two level indices differ by more than 2; diagonal entries 1 or more.
All inputs are finite; a program needn't handle non-finite values.
Results may differ from a plain program's by a relative error of at most 0.0049.
Values may be sent and summed in bfloat16 or wider, within the bound.
A program may use at most 64 MiB of HBM per device.

v0:
```python
import math

import jax
import jax.numpy as jnp
from jax import lax
from jax.sharding import PartitionSpec as P


def fourier_basis(waves, length):
    points = lax.broadcasted_iota(jnp.int32, (length, waves.shape[0]), 0)
    phases = points * waves[None, :] % length
    angles = phases.astype(jnp.float32) * jnp.float32(2.0 * math.pi / length)
    factor = jnp.float32(math.sqrt(2.0 / length))
    return jnp.concatenate([jnp.cos(angles) * factor, -jnp.sin(angles) * factor], axis=1).astype(
        jnp.bfloat16
    )


def on_device(grid_field, lon_count, wave_table, legendre, vertical):
    lat_devices = lax.axis_size("lat")
    lev_devices = lax.axis_size("lev")
    lat_rows, lev_rows, lon_points = grid_field.shape
    wave_count = wave_table.shape[0]
    per_device = wave_count // (lat_devices * lev_devices)
    basis = fourier_basis(wave_table, lon_points)
    fourier = jnp.dot(
        grid_field.reshape(lat_rows * lev_rows, lon_points),
        basis,
        preferred_element_type=jnp.float32,
    )
    fourier = fourier.reshape(lat_rows, lev_rows, 2, wave_count)
    retained = 2 * wave_table[None, :] < lon_count[:, None]
    fourier = jnp.where(retained[:, None, None, :], fourier, 0.0).astype(jnp.bfloat16)
    received = lax.all_to_all(
        lax.all_to_all(fourier, "lat", split_axis=3, concat_axis=0, tiled=True),
        "lev",
        split_axis=3,
        concat_axis=1,
        tiled=True,
    )
    half_lat = received.shape[0] // 2
    northern_rows = received[:half_lat].astype(jnp.float32)
    southern_rows = received[half_lat:][::-1].astype(jnp.float32)
    symmetric = (northern_rows + southern_rows).astype(jnp.bfloat16)
    antisym = (northern_rows - southern_rows).astype(jnp.bfloat16)
    group_index = lax.axis_index("lat") * lev_devices + lax.axis_index("lev")
    local_waves = lax.dynamic_slice_in_dim(wave_table, group_index * per_device, per_device)
    half_waves = wave_count // 2
    even_part = jnp.einsum(
        "slq,lvcs->vcsq", legendre[:, :, :half_waves], symmetric, preferred_element_type=jnp.float32
    )
    odd_part = jnp.einsum(
        "slq,lvcs->vcsq", legendre[:, :, half_waves:], antisym, preferred_element_type=jnp.float32
    )
    projected = jnp.concatenate([even_part, odd_part], axis=3)
    degree = jnp.arange(wave_count, dtype=jnp.int32)
    offset = jnp.where(degree < half_waves, 2 * degree, 2 * (degree - half_waves) + 1)
    in_range = local_waves[:, None] + offset[None, :] < wave_count
    projected = jnp.where(in_range[None, None], projected, 0.0)
    return jnp.einsum("wv,wcsq->vcsq", vertical, projected, precision=lax.Precision.HIGHEST)


def solution(mesh):
    return jax.shard_map(
        on_device,
        mesh=mesh,
        in_specs=(P("lat", "lev", None), P("lat"), P(), P(("lat", "lev"), None, None), P()),
        out_specs=P(None, None, ("lat", "lev"), None),
        check_vma=False,
    )
```

profile of v0, /device:TPU:1, one launch (start us, length us, event | category | flops | bytes accessed | tf_op | source)
XLA Modules:
  0.0 219.7 jit_solution(13937160845294109802)
XLA Ops:
  0.0 0.0 copy-start
  0.0 0.0 copy-start.3
  0.0 56.3 %multiply_convert_fusion.1 = (bf16[2560,1280]{1,0:T(8,128)(2,1)S(1)}, bf16[2560,1280]{1,0:T(8,128)(2,1)S(1)}) fusion(s32[1280]{0:T(1024)} %param.7), kind=kLoop, calls=%fused_computation.8 | loop fusion | flops 45875200 | bytes 13112320 | tf_op jit(solution)/shard_map/convert.1
  56.3 0.0 copy-done.3
  56.4 0.0 copy-done
  56.4 6.8 %fusion.2 = bf16[2560,320]{0,1:T(8,128)(2,1)} fusion(bf16[2560,1280]{1,0:T(8,128)(2,1)S(1)} %get-tuple-element.8, bf16[2560,1280]{1,0:T(8,128)(2,1)S(1)} %get-tuple-element.7, bf16[40,8,2560]{2,1,0:T(8,128)(2,1)S(1)} %copy-done), kind=kOutput, calls=%fused_computation.3 | convolution fusion | flops 4220518400 | bytes 16384000 | tf_op jit(solution)/shard_map/dot_general | solution.py:26
  63.2 0.0 copy-start.4
  63.2 9.0 %copy.28 = bf16[40,8,2,1280]{0,1,2,3:T(8,128)(2,1)} copy(bf16[40,8,2,1280]{3,1,2,0:T(8,128)(2,1)} %bitcast.50) | data formatting | bytes 3276800 | tf_op jit(solution)/shard_map/reshape | solution.py:31
  72.1 0.0 copy-done.4
  72.1 0.2 broadcast_compare_fusion
  72.4 7.8 %fusion.37 = bf16[1280,2,8,40]{3,2,1,0:T(8,128)(2,1)} fusion(bf16[40,8,2,1280]{0,1,2,3:T(8,128)(2,1)} %copy.28, pred[40,1280]{0,1:T(8,128)(4,1)S(1)} %broadcast_compare_fusion), kind=kLoop, calls=%fused_computation.48 | loop fusion | flops 819200 | bytes 3328000
  80.2 10.9 %reshape.80 = bf16[32,2,12800]{2,1,0:T(2,128)(2,1)S(1)} reshape(bf16[1280,2,8,40]{3,2,1,0:T(8,128)(2,1)} %fusion.37) | data formatting | bytes 3276800
  91.1 31.9 %all_to_all.33 = bf16[32,2,12800]{2,1,0:T(2,128)(2,1)S(1)} all-to-all(bf16[32,2,12800]{2,1,0:T(2,128)(2,1)S(1)} %reshape.80), channel_id=1, replica_groups=mesh['lat'=32,'lev'=8] {'lat'}, dimensions={0} | all-to-all | bytes 3276800 | tf_op jit(solution)/shard_map/all_to_all | solution.py:35
  123.0 9.3 %reshape.81 = bf16[1280,2,8,40]{3,2,1,0:T(8,128)(2,1)} reshape(bf16[32,2,12800]{2,1,0:T(2,128)(2,1)S(1)} %all_to_all.33) | data formatting | bytes 3276800
  132.3 10.9 %copy.40 = bf16[32,40,8,2,40]{1,0,3,2,4:T(8,128)(2,1)} copy(bf16[32,40,8,2,40]{1,2,3,4,0:T(8,128)(2,1)} %bitcast.47) | data formatting | bytes 3276800 | tf_op jit(solution)/shard_map/all_to_all | solution.py:35
  143.2 11.2 %reshape.79 = bf16[1280,8,2,40]{0,2,1,3:T(2,128)(2,1)} reshape(bf16[32,40,8,2,40]{1,0,3,2,4:T(8,128)(2,1)} %copy.40) | data formatting | bytes 3276800 | tf_op jit(solution)/shard_map/all_to_all | solution.py:35
  154.4 8.2 %all-to-all-start.1 = ((bf16[1280,8,2,40]{0,2,1,3:T(2,128)(2,1)}), bf16[1280,8,2,40]{0,2,1,3:T(2,128)(2,1)S(1)}, u32[]{:S(2)}, u32[]{:S(2)}) async-start(bf16[1280,8,2,40]{0,2,1,3:T(2,128)(2,1)} %reshape.79), calls=%async_computation.1 | async-start | bytes 3276800 | tf_op jit(solution)/shard_map/all_to_all | solution.py:34
  162.6 0.1 dynamic_slice.3
  162.7 0.1 add_compare_fusion
  162.8 41.7 %all-to-all-done.1 = bf16[1280,8,2,40]{0,2,1,3:T(2,128)(2,1)S(1)} async-done(((bf16[1280,8,2,40]{0,2,1,3:T(2,128)(2,1)}), bf16[1280,8,2,40]{0,2,1,3:T(2,128)(2,1)S(1)}, u32[]{:S(2)}, u32[]{:S(2)}) %all-to-all-start.1) | async-done | bytes 1638432 | tf_op jit(solution)/shard_map/all_to_all | solution.py:34
  204.5 0.2 copy.32
  204.7 0.2 slice_convert_fusion
  204.8 0.1 copy.48
  204.9 0.9 rev.3
  205.8 3.1 %fusion.25 = f32[64,2,5,640]{3,0,2,1:T(8,128)S(1)} fusion(bf16[5,640,1280]{2,1,0:T(8,128)(2,1)} %param.8, bf16[640,64,2,5]{0,1,3,2:T(8,128)(2,1)S(1)} %rev.3, f32[640,8,8,2,5]{0,2,4,1,3:T(8,128)S(1)} %get-tuple-element.5), kind=kOutput, calls=%fused_computation.32 | convolution fusion | flops 525516800 | bytes 8192000 | tf_op jit(solution)/shard_map/slq,lvcs->vcsq/dot_general | solution.py:52
  208.9 0.0 copy-start.2
  208.9 3.1 %fusion.22 = f32[64,2,5,640]{3,0,2,1:T(8,128)S(1)} fusion(bf16[5,640,1280]{2,1,0:T(8,128)(2,1)} %param.8, bf16[640,64,2,5]{0,1,3,2:T(8,128)(2,1)S(1)} %rev.3, f32[640,8,8,2,5]{0,2,4,1,3:T(8,128)S(1)} %get-tuple-element.5), kind=kOutput, calls=%fused_computation.31 | convolution fusion | flops 525516800 | bytes 8192000 | tf_op jit(solution)/shard_map/slq,lvcs->vcsq/dot_general | solution.py:49
  212.1 0.0 copy-done.2
  212.1 0.0 copy-start.1
  212.1 3.4 %convolution_bitcast_fusion = f32[64,2,5,1280]{3,0,2,1:T(8,128)S(1)} fusion(f32[64,2,5,640]{3,0,2,1:T(8,128)S(1)} %fusion.25, f32[64,2,5,640]{3,0,2,1:T(8,128)S(1)} %fusion.22, pred[5,1280]{1,0:T(8,128)(4,1)S(1)} %add_compare_fusion, f32[64,64]{1,0:T(8,128)S(1)} %copy-done.2), kind=kOutput, calls=%fused_computation.20 | convolution fusion | flops 630784000 | bytes 6576384 | tf_op jit(solution)/shard_map/wv,wcsq->vcsq/dot_general | solution.py:60
  215.4 4.2 %copy.36 = f32[64,2,5,1280]{3,1,2,0:T(2,128)} copy(f32[64,2,5,1280]{3,0,2,1:T(8,128)S(1)} %convolution_bitcast_fusion) | data formatting | bytes 6553600 | tf_op jit(solution)/shard_map/wv,wcsq->vcsq/dot_general | solution.py:60
  219.7 0.0 copy-done.1
  (2 shorter events, 0.0 us)
Async XLA Ops:
  0.0 56.4 %copy-start = (bf16[40,8,2560]{2,1,0:T(8,128)(2,1)S(1)}, bf16[40,8,2560]{2,1,0:T(8,128)(2,1)}, u32[]{:S(2)}) copy-start(bf16[40,8,2560]{2,1,0:T(8,128)(2,1)} %param.5) | copy-start | bytes 4915204
  0.0 56.3 %copy-start.3 = (s32[1280]{0:T(1024)S(1)}, s32[1280]{0:T(1024)}, u32[]{:S(2)}) copy-start(s32[1280]{0:T(1024)} %param.7) | copy-start | bytes 15364
  63.2 9.0 %copy-start.4 = (s32[40]{0:T(128)S(1)}, s32[40]{0:T(128)}, u32[]{:S(2)}) copy-start(s32[40]{0:T(128)} %param.6) | copy-start | bytes 484
  154.4 50.1 %all-to-all-start.1 = ((bf16[1280,8,2,40]{0,2,1,3:T(2,128)(2,1)}), bf16[1280,8,2,40]{0,2,1,3:T(2,128)(2,1)S(1)}, u32[]{:S(2)}, u32[]{:S(2)}) async-start(bf16[1280,8,2,40]{0,2,1,3:T(2,128)(2,1)} %reshape.79), calls=%async_computation.1 | async-start | bytes 3276800 | tf_op jit(solution)/shard_map/all_to_all | solution.py:34
  208.9 3.1 %copy-start.2 = (f32[64,64]{1,0:T(8,128)S(1)}, f32[64,64]{1,0:T(8,128)}, u32[]{:S(2)}) copy-start(f32[64,64]{1,0:T(8,128)} %param.9) | copy-start | bytes 49156
  212.1 7.6 %copy-start.1 = (bf16[40,8,2560]{2,1,0:T(8,128)(2,1)S(1)}, bf16[40,8,2560]{2,1,0:T(8,128)(2,1)}, u32[]{:S(2)}) copy-start(bf16[40,8,2560]{2,1,0:T(8,128)(2,1)} %param.5) | copy-start | bytes 4915204
where the time goes:
time: 220 us
  other arithmetic  64.6 us (29%)
  local copies, waits for them, and re-layouts  56.8 us (26%)
  waiting for transfers between devices  41.7 us (19%)
  blocking collectives  31.9 us (14%)
  matrix products  16.4 us (7%)
  starting transfers between devices  8.18 us (4%)
    another operation x1, other arithmetic  56.3 us
    all_to_all x1, waiting for transfers between devices, on_device(): lax.all_to_all(lax.all_to_all(fourier, 'lat', split_axis=3, concat_axis=0...  41.7 us
    all_to_all x1, blocking collectives, on_device(): lax.all_to_all(fourier, 'lat', split_axis=3, concat_axis=0, tiled=True)  31.9 us
    all_to_all x2, local copies, waits for them, and re-layouts, on_device(): lax.all_to_all(fourier, 'lat', split_axis=3, concat_axis=0, tiled=True)  22.1 us
    unnamed x12, local copies, waits for them, and re-layouts  20.2 us
    reshape x1, local copies, waits for them, and re-layouts, on_device(): fourier = fourier.reshape(lat_rows, lev_rows, 2, wave_count)  8.97 us
    all_to_all x1, starting transfers between devices, on_device(): lax.all_to_all(lax.all_to_all(fourier, 'lat', split_axis=3, concat_axis=0...  8.18 us
    unnamed x1, other arithmetic  7.8 us
  transfers between devices with their start and end apart: 1, of which 1 were waited for; matrix products, arithmetic and copies ran while one was open for 0% of the time, Pallas kernels for 0%

commit v1 on v0

v1 whole, which is shorter than its diff:
```python
import functools
import math

import jax
import jax.numpy as jnp
import ml_dtypes
import numpy as np
from jax import lax
from jax.experimental import pallas as pl
from jax.experimental.pallas import tpu as pltpu
from jax.sharding import PartitionSpec as P

MESH = pl.DeviceIdType.MESH
NLON = 2560
NT = 1280
HALF = 640
ROUNDS = 5
WAVES = 256
LATS = 32
LEVS = 8
ROWS = 40
PAD = 48
NV = 8
F32 = jnp.float32
BF16 = jnp.bfloat16


def basis_constant():
    points = np.arange(NLON, dtype=np.int64)
    column = np.arange(WAVES, dtype=np.int64)
    factor = np.float32(math.sqrt(2.0 / NLON))
    rounds = []
    for r in range(ROUNDS):
        waves = r * WAVES + (column if r % 2 == 0 else WAVES - 1 - column)
        phases = points[:, None] * waves[None, :] % NLON
        angles = phases.astype(np.float32) * np.float32(2.0 * math.pi / NLON)
        rounds.append(np.concatenate([np.cos(angles) * factor, -np.sin(angles) * factor], axis=1))
    return np.stack(rounds).astype(ml_dtypes.bfloat16)


def iota(shape, dim):
    return lax.broadcasted_iota(jnp.int32, shape, dim)


def one_hot(mask):
    return jnp.where(mask, 1.0, 0.0).astype(BF16)


def dot(a, b):
    return jnp.dot(a, b, preferred_element_type=F32)


def dot_nt(a, b):
    return lax.dot_general(a, b, (((1,), (1,)), ((), ())), preferred_element_type=F32)


def kernel(
    wave_ref, lon_ref, target_ref, vertical_ref, grid_ref, basis_ref, legendre_ref,
    out_ref,
    x, basis, table, lon, route, order, mix, folded, sent, got, turned, ready, result,
    in_sem, basis_sem, table_sem, out_sem, lat_send, lat_recv, lev_send, lev_recv,
):
    me = lax.axis_index("lat")
    lev = lax.axis_index("lev")

    grid_copy = pltpu.make_async_copy(grid_ref, x, in_sem)
    grid_copy.start()
    basis_copies = [pltpu.make_async_copy(basis_ref.at[r], basis.at[r], basis_sem.at[r]) for r in range(ROUNDS)]
    for copy in basis_copies:
        copy.start()
    table_copies = []
    for r in range(ROUNDS):
        width = HALF - 128 * r
        for part in range(2):
            block = (r, slice(None), pl.ds(part * HALF, width))
            table_copies.append(
                pltpu.make_async_copy(legendre_ref.at[block], table.at[block], table_sem.at[r, part])
            )
    for copy in table_copies:
        copy.start()

    barrier = pltpu.get_barrier_semaphore()

    def greet_lat(k, carry):
        pl.semaphore_signal(barrier, inc=1, device_id=(lax.rem(me + k, LATS), lev), device_id_type=MESH)
        return carry

    def greet_lev(k, carry):
        pl.semaphore_signal(barrier, inc=1, device_id=(me, lax.rem(lev + k, LEVS)), device_id_type=MESH)
        return carry

    lax.fori_loop(1, LATS, greet_lat, 0)
    lax.fori_loop(1, LEVS, greet_lev, 0)

    for t in range(ROWS):
        lon[pl.ds(t * NV, NV), :] = jnp.full((NV, 128), lon_ref[t], jnp.int32)
    route[...] = one_hot(iota((2 * WAVES, 2 * WAVES), 0) == target_ref[...])
    row = iota((NV * PAD, ROWS * NV), 0)
    col = iota((NV * PAD, ROWS * NV), 1)
    at = lax.rem(row, PAD)
    at = jnp.where(me < LATS // 2, at, ROWS - 1 - at)
    order[...] = one_hot((lax.div(col, NV) == at) & (lax.rem(col, NV) == lax.div(row, PAD)))

    lane_block = lax.div(iota((PAD, 128), 1), 16)

    def send_lat(r):
        def start(k, carry):
            peer = lax.rem(me + k, LATS)
            pltpu.make_async_remote_copy(
                src_ref=sent.at[r, peer],
                dst_ref=got.at[r, me],
                send_sem=lat_send.at[r],
                recv_sem=lat_recv.at[r],
                device_id=(peer, lev),
                device_id_type=MESH,
            ).start()
            return carry

        lax.fori_loop(1, LATS, start, 0)

    def fourier(r):
        values = dot(x[...].reshape(ROWS * NV, NLON), basis[r])
        column = iota((8, 2 * WAVES), 1) & (WAVES - 1)
        odd = lax.rem(r, 2) == 1
        waves = r * WAVES + jnp.where(odd, WAVES - 1 - column, column)
        twice = jnp.broadcast_to(2 * waves[:1], (ROWS * NV, 2 * WAVES))
        longitudes = jnp.concatenate([lon[...]] * 4, axis=1)
        values = jnp.where(twice < longitudes, values, 0.0).astype(BF16)
        values = dot(order[...], values).astype(BF16)
        values = dot(values, route[...])
        for high in range(LATS // 8):
            blocks = []
            for v in range(NV):
                block = values[v * PAD : (v + 1) * PAD, high * 128 : (high + 1) * 128]
                blocks.append(pltpu.roll(block, 16 * v, 1) if v else block)
            for bit in range(3):
                taken = (lane_block >> bit) & 1 == 1
                blocks = [jnp.where(taken, blocks[(i + (1 << bit)) % 8], blocks[i]) for i in range(8)]
            for low in range(8):
                sent[r, high * 8 + low] = blocks[-low % 8].astype(BF16)

    def turn(r):
        pltpu.make_async_copy(got.at[r, pl.ds(0, LATS - 1)], got.at[r, pl.ds(0, LATS - 1)], lat_recv.at[r]).wait()
        got[r, me] = sent[r, me]
        for i in range(LATS // 2):
            north = got[r, i].astype(F32)[:ROWS]
            south = got[r, LATS - 1 - i].astype(F32)[:ROWS]
            folded[0, pl.ds(i * ROWS, ROWS), :] = north + south
            folded[1, pl.ds(i * ROWS, ROWS), :] = north - south
        row = iota((128, 128), 0)
        col = iota((128, 128), 1)
        level = row & 7
        source = 16 * ((level + me) & 7) + 8 * ((row >> 3) & 1) + (row >> 4)
        pick = one_hot(col == source)
        for part in range(2):
            values = dot_nt(pick, folded[part].astype(BF16)).astype(BF16)
            turned[r, :, :, pl.ds(part * HALF, HALF)] = values.reshape(LEVS, 16, HALF)

        def start(k, carry):
            peer = lax.rem(lev + k, LEVS)
            pltpu.make_async_remote_copy(
                src_ref=turned.at[r, peer],
                dst_ref=ready.at[r, lev],
                send_sem=lev_send.at[r],
                recv_sem=lev_recv.at[r],
                device_id=(me, peer),
                device_id_type=MESH,
            ).start()
            return carry

        lax.fori_loop(1, LEVS, start, 0)

    def vertical_operator():
        row = iota((128, 64), 0)
        pick_out = one_hot(iota((128, 64), 1) == (row >> 1))
        col = iota((64, 128), 1)
        pick_in = one_hot(iota((64, 128), 0) == 8 * (col >> 4) + (col & 7))
        same = (iota((128, 128), 0) & 1) == ((iota((128, 128), 1) >> 3) & 1)
        whole = vertical_ref[...]
        high = whole.astype(BF16)
        low = (whole - high.astype(F32)).astype(BF16)
        for k, term in enumerate((high, low)):
            term = dot_nt(pick_out, term).astype(BF16)
            term = dot(term, pick_in)
            mix[:, pl.ds(128 * k, 128)] = jnp.where(same, term, 0.0).astype(BF16)

    def legendre(r):
        pltpu.make_async_copy(ready.at[r, pl.ds(0, LEVS - 1)], ready.at[r, pl.ds(0, LEVS - 1)], lev_recv.at[r]).wait()
        ready[r, lev] = turned[r, lev]
        width = HALF - 128 * r
        wave = wave_ref[(me * LEVS + lev) * ROUNDS + r]
        table_copies[2 * r].wait()
        table_copies[2 * r + 1].wait()
        values = ready[r].reshape(128, NT)
        mixed = dot(mix[...], jnp.concatenate([values, values], axis=0)).astype(BF16)
        for part in range(2):
            total = dot(mixed[:, part * HALF : (part + 1) * HALF], table[r, :, pl.ds(part * HALF, width)])
            degree = wave + 2 * iota((128, width), 1) + part
            result[r, :, pl.ds(part * HALF, width)] = jnp.where(degree < NT, total, 0.0)
            if width < HALF:
                result[r, :, pl.ds(part * HALF + width, HALF - width)] = jnp.zeros((128, HALF - width), F32)
        pltpu.make_async_copy(result.at[r], out_ref.at[r], out_sem.at[r]).start()

    grid_copy.wait()
    basis_copies[0].wait()
    fourier(0)
    pl.semaphore_wait(barrier, LATS - 1 + LEVS - 1)
    send_lat(0)
    vertical_operator()

    def step(r, carry):
        pltpu.make_async_copy(basis_ref.at[r], basis.at[r], basis_sem.at[r]).wait()
        fourier(r)
        send_lat(r)
        turn(r - 1)
        return carry

    lax.fori_loop(1, ROUNDS, step, 0)
    legendre(0)
    turn(ROUNDS - 1)
    for r in range(1, ROUNDS):
        legendre(r)
    for r in range(ROUNDS):
        pltpu.make_async_copy(result.at[r], out_ref.at[r], out_sem.at[r]).wait()
        pltpu.make_async_copy(sent.at[r, pl.ds(0, LATS - 1)], sent.at[r, pl.ds(0, LATS - 1)], lat_send.at[r]).wait()
        pltpu.make_async_copy(turned.at[r, pl.ds(0, LEVS - 1)], turned.at[r, pl.ds(0, LEVS - 1)], lev_send.at[r]).wait()


def on_device(grid_field, lon_count, wave_table, legendre, vertical):
    place = wave_table[::ROUNDS].reshape(LATS, 1, LEVS)
    target = place + WAVES * jnp.arange(2, dtype=jnp.int32)[None, :, None]
    anywhere = pl.BlockSpec(memory_space=pl.ANY)
    vmem = pl.BlockSpec(memory_space=pltpu.VMEM)
    smem = pl.BlockSpec(memory_space=pltpu.SMEM)
    result = pl.pallas_call(
        kernel,
        out_shape=jax.ShapeDtypeStruct((ROUNDS, 128, NT), F32),
        in_specs=[smem, smem, vmem, vmem, anywhere, anywhere, anywhere],
        out_specs=anywhere,
        scratch_shapes=[
            pltpu.VMEM((ROWS, NV, NLON), BF16),
            pltpu.VMEM((ROUNDS, NLON, 2 * WAVES), BF16),
            pltpu.VMEM((ROUNDS, HALF, NT), BF16),
            pltpu.VMEM((ROWS * NV, 128), jnp.int32),
            pltpu.VMEM((2 * WAVES, 2 * WAVES), BF16),
            pltpu.VMEM((NV * PAD, ROWS * NV), BF16),
            pltpu.VMEM((128, 256), BF16),
            pltpu.VMEM((2, HALF, 128), F32),
            pltpu.VMEM((ROUNDS, LATS, PAD, 128), BF16),
            pltpu.VMEM((ROUNDS, LATS, PAD, 128), BF16),
            pltpu.VMEM((ROUNDS, LEVS, 16, NT), BF16),
            pltpu.VMEM((ROUNDS, LEVS, 16, NT), BF16),
            pltpu.VMEM((ROUNDS, 128, NT), F32),
            pltpu.SemaphoreType.DMA,
            pltpu.SemaphoreType.DMA((ROUNDS,)),
            pltpu.SemaphoreType.DMA((ROUNDS, 2)),
            pltpu.SemaphoreType.DMA((ROUNDS,)),
            pltpu.SemaphoreType.DMA((ROUNDS,)),
            pltpu.SemaphoreType.DMA((ROUNDS,)),
            pltpu.SemaphoreType.DMA((ROUNDS,)),
            pltpu.SemaphoreType.DMA((ROUNDS,)),
        ],
        compiler_params=pltpu.CompilerParams(collective_id=0, has_side_effects=True, vmem_limit_bytes=56 << 20),
        cost_estimate=pl.CostEstimate(flops=6_000_000_000, bytes_accessed=24_000_000, transcendentals=0),
    )(wave_table, lon_count, target.reshape(1, 2 * WAVES), vertical, grid_field, jnp.asarray(basis_constant()), legendre)
    return result.reshape(ROUNDS, 64, 2, NT).transpose(1, 2, 0, 3)


def solution(mesh):
    return jax.shard_map(
        on_device,
        mesh=mesh,
        in_specs=(P("lat", "lev", None), P("lat"), P(), P(("lat", "lev"), None, None), P()),
        out_specs=P(None, None, ("lat", "lev"), None),
        check_vma=False,
    )
```

time: 220 us -> 73.9 us (0.34)
  the two profiles are of different devices: /device:TPU:1 before, /device:TPU:7 now
where the time goes in v1:
time: 73.9 us; the launch traced here: 73.7 us
  Pallas kernels  65.3 us (88%)
  local copies, waits for them, and re-layouts  8.3 us (11%)
    pallas_call x1, Pallas kernels, on_device(): pl.pallas_call(kernel, out_shape=jax.ShapeDtypeStruct((ROUNDS, 128, NT),...  65.3 us
    reshape x2, local copies, waits for them, and re-layouts, on_device(): return result.reshape(ROUNDS, 64, 2, NT).transpose(1, 2, 0, 3)  6.7 us

profile of v1, /device:TPU:7, one launch (start us, length us, event | category | flops | bytes accessed | tf_op | source)
XLA Modules:
  0.0 73.7 jit_solution(11141276675134456623)
XLA Ops:
  0.0 0.8 %slice.3 = s32[256]{0:T(256)S(1)} slice(s32[1280]{0:T(1024)} %wave_ref.1), slice={[0:1280:5]} | slice | bytes 2048 | tf_op jit(solution)/shard_map/slice | solution.py:230
  0.8 0.1 add.25
  0.9 0.1 broadcast_add_fusion
  1.0 0.7 add.29.target_ref
  1.7 65.3 %shard_map.64 = f32[5,128,1280]{2,1,0:T(8,128)} custom-call(s32[1280]{0:T(1024)} %wave_ref.1, s32[40]{0:T(128)} %lon_ref.1, s32[1,512]{1,0:T(1,128)} %add.29.target_ref, f32[64,64]{1,0:T(8,128)} %vertical_ref.1, bf16[40,8,2560]{2,1,0:T(8,128)(2,1)} %grid_ref.1, bf16[5,2560,512]{2,1,0:T(8,128)(2,1)} %constant.4.clone.basis_ref, bf16[5,640,1280]{2,1,0:T(8,128)(2,1)} %legendre_ref.1), custom_call_target="tpu_custom_call" | custom-call | flops 6000000000 | bytes 24000000 | tf_op jit(solution)/shard_map/pallas_call | solution.py:235
  67.0 3.9 %reshape.33 = f32[5,64,2,1280]{3,2,1,0:T(2,128)S(1)} reshape(f32[5,128,1280]{2,1,0:T(8,128)} %shard_map.64) | data formatting | bytes 6553600 | tf_op jit(solution)/shard_map/reshape | solution.py:266
  70.9 2.8 %copy.10 = f32[5,64,2,1280]{3,2,0,1:T(2,128)} copy(f32[5,64,2,1280]{3,2,1,0:T(2,128)S(1)} %reshape.33) | data formatting | bytes 6553600 | tf_op jit(solution)/shard_map/reshape | solution.py:266
  (1 shorter events, 0.0 us)

commit v2 on v1

v2 whole, which is shorter than its diff:
```python
import functools
import math

import jax
import jax.numpy as jnp
import ml_dtypes
import numpy as np
from jax import lax
from jax.experimental import pallas as pl
from jax.experimental.pallas import tpu as pltpu
from jax.sharding import PartitionSpec as P

MESH = pl.DeviceIdType.MESH
NLON = 2560
NT = 1280
HALF = 640
ROUNDS = 5
WAVES = 256
LATS = 32
LEVS = 8
ROWS = 40
PAD = 48
NV = 8
EDGE = 16
POLAR = 7
F32 = jnp.float32
BF16 = jnp.bfloat16


class Plan:
    def __init__(self, sparse):
        self.sparse = sparse
        if sparse:
            self.first_pair = [0] + [(128 * r - EDGE) // ROWS for r in range(1, ROUNDS)]
            self.chunks = [(0, 0, 256), (4, 512, HALF), (3, 384, HALF), (2, 256, HALF), (1, 128, HALF), (0, 256, HALF)]
            self.turn_step = [1, 1, 2, 3, 4, 5]
        else:
            self.first_pair = [0] * ROUNDS
            self.chunks = [(r, 0, HALF) for r in range(ROUNDS)]
            self.turn_step = [r + 1 for r in range(ROUNDS)]

    def pairs(self, chunk):
        r, low, high = self.chunks[chunk]
        edge = EDGE if self.sparse and r else 0
        return range((low - edge) // ROWS, -(-high // ROWS))

    def sources(self, chunk):
        r = self.chunks[chunk][0]
        if self.sparse and r == 0:
            return (0, POLAR) if chunk == 0 else (POLAR, LATS // 2)
        return (self.first_pair[r], LATS // 2)

    def table_start(self, r):
        return 128 * max(r - 1, 0) if self.sparse else 0


def basis_constant():
    points = np.arange(NLON // 2, dtype=np.int64)
    column = np.arange(WAVES, dtype=np.int64)
    factor = np.float32(math.sqrt(2.0 / NLON))
    rounds = []
    for r in range(ROUNDS):
        waves = r * WAVES + (column if r % 2 == 0 else WAVES - 1 - column)
        phases = points[:, None] * waves[None, :] % NLON
        angles = phases.astype(np.float32) * np.float32(2.0 * math.pi / NLON)
        cosines, sines = np.cos(angles) * factor, -np.sin(angles) * factor
        rounds.append(np.concatenate([cosines[:, 0::2], sines[:, 0::2], cosines[:, 1::2], sines[:, 1::2]], axis=1))
    return np.stack(rounds).astype(ml_dtypes.bfloat16)


def iota(shape, dim):
    return lax.broadcasted_iota(jnp.int32, shape, dim)


def one_hot(mask):
    return jnp.where(mask, 1.0, 0.0).astype(BF16)


def dot(a, b):
    return jnp.dot(a, b, preferred_element_type=F32)


def dot_nt(a, b):
    return lax.dot_general(a, b, (((1,), (1,)), ((), ())), preferred_element_type=F32)


def await_bytes(ref, semaphore):
    pltpu.make_async_copy(ref, ref, semaphore).wait()


def kernel(plan, *refs):
    (
        wave_ref, lon_ref, wave_row_ref, vertical_ref, grid_ref, basis_ref, legendre_ref,
        out_ref, flag_ref,
        x, basis, table, lon, route, order, mix, folded, edges, sent, got, edge_sent, edge_got, result, *chunk_refs,
    ) = refs
    count = len(plan.chunks)
    turned, ready = chunk_refs[:count], chunk_refs[count : 2 * count]
    (
        in_sem, basis_sem, table_sem, out_sem, lat_send, lat_recv, lev_send, lev_recv, edge_send, edge_recv,
    ) = chunk_refs[2 * count :]
    me = lax.axis_index("lat")
    lev = lax.axis_index("lev")
    pair = jnp.minimum(me, LATS - 1 - me)

    def sends(r):
        first = 0
        for k in range(1, ROUNDS):
            first = jnp.where(r == k, plan.first_pair[k], first)
        return pair >= first

    def round_at(step):
        if not plan.sparse:
            return step, step < ROUNDS
        usual = ROUNDS - 1 - step
        early = (pair < POLAR) & (step == 0)
        r = jnp.where(early, 0, usual)
        due = early | ((step > 0) | (pair >= POLAR)) & sends(usual) & ~((pair < POLAR) & (usual == 0))
        return jnp.maximum(r, 0), due & (usual >= 0)

    def basis_copy(r):
        return pltpu.make_async_copy(basis_ref.at[r], basis.at[r], basis_sem.at[r])

    grid_copy = pltpu.make_async_copy(grid_ref, x, in_sem)
    grid_copy.start()

    def start_basis(step, carry):
        r, due = round_at(step)

        @pl.when(due)
        def _():
            basis_copy(r).start()

        return carry

    lax.fori_loop(0, ROUNDS, start_basis, 0)
    table_copies = {}
    for r in reversed(range(ROUNDS)):
        start, width = plan.table_start(r), HALF - 128 * r
        for part in range(2):
            block = (r, pl.ds(start, HALF - start), pl.ds(part * HALF, width))
            copy = pltpu.make_async_copy(legendre_ref.at[block], table.at[block], table_sem.at[r, part])
            copy.start()
            table_copies[r, part] = copy

    barrier = pltpu.get_barrier_semaphore()

    def greet_lat(k, carry):
        pl.semaphore_signal(barrier, inc=1, device_id=(lax.rem(me + k, LATS), lev), device_id_type=MESH)
        return carry

    def greet_lev(k, carry):
        pl.semaphore_signal(barrier, inc=1, device_id=(me, lax.rem(lev + k, LEVS)), device_id_type=MESH)
        return carry

    lax.fori_loop(1, LATS, greet_lat, 0)
    lax.fori_loop(1, LEVS, greet_lev, 0)

    for t in range(ROWS):
        lon[pl.ds(t * NV, NV), :] = jnp.full((NV, 128), lon_ref[t], jnp.int32)
    row = iota((NT, 2 * WAVES), 0)
    col = iota((NT, 2 * WAVES), 1)
    pick = one_hot(row == ROUNDS * (8 * (col >> 4) + (col & 7)))
    waves = jnp.broadcast_to(wave_row_ref[...].astype(F32), (8, NT)).astype(BF16)
    place = dot(waves, pick).astype(jnp.int32)
    target = WAVES * (place & 1) + 128 * ((iota((8, 2 * WAVES), 1) >> 3) & 1) + (place >> 1)
    route[...] = one_hot(iota((2 * WAVES, 2 * WAVES), 0) == target[:1])
    row = iota((NV * PAD, ROWS * NV), 0)
    col = iota((NV * PAD, ROWS * NV), 1)
    at = lax.rem(row, PAD)
    at = jnp.where(me < LATS // 2, at, ROWS - 1 - at)
    order[...] = one_hot((lax.div(col, NV) == at) & (lax.rem(col, NV) == lax.div(row, PAD)))
    latitude = me * ROWS + lax.div(iota((ROWS * NV, 128), 0), NV)
    latitude = jnp.minimum(latitude, NT - 1 - latitude)
    over = jnp.where(lon[...] > 512 * (((latitude + EDGE) >> 7) + 1), 1.0, 0.0)
    over = jnp.broadcast_to(jnp.max(over, axis=0, keepdims=True), (PAD - ROWS, 128))
    flag_ref[...] = over
    folded[...] = jnp.zeros_like(folded)
    edges[...] = jnp.zeros_like(edges)

    lane_block = lax.div(iota((PAD, 128), 1), 16)

    def fourier(r):
        odd = lax.rem(r, 2)
        first = dot(x[:, :, : NLON // 2].reshape(ROWS * NV, NLON // 2), basis[r])
        second = dot(x[:, :, NLON // 2 :].reshape(ROWS * NV, NLON // 2), basis[r])
        values = first + second * jnp.where((iota((1, 2 * WAVES), 1) >> 8) == odd, 1.0, -1.0)
        column = iota((8, 2 * WAVES), 1)
        column = 2 * (column & 127) + (column >> 8)
        waves = r * WAVES + jnp.where(odd == 1, WAVES - 1 - column, column)
        twice = jnp.broadcast_to(2 * waves[:1], (ROWS * NV, 2 * WAVES))
        longitudes = jnp.concatenate([lon[...]] * 4, axis=1)
        values = jnp.where(twice < longitudes, values, 0.0).astype(BF16)
        values = dot(order[...], values).astype(BF16)
        values = dot(values, route[...])
        for high in range(LATS // 8):
            blocks = []
            for v in range(NV):
                block = values[v * PAD : (v + 1) * PAD, high * 128 : (high + 1) * 128]
                blocks.append(pltpu.roll(block, 16 * v, 1) if v else block)
            for bit in range(3):
                taken = (lane_block >> bit) & 1 == 1
                blocks = [jnp.where(taken, blocks[(i + (1 << bit)) % 8], blocks[i]) for i in range(8)]
            for low in range(8):
                block = jnp.concatenate([blocks[-low % 8][:ROWS], over], axis=0)
                sent[r, high * 8 + low] = block.astype(BF16)

    def send_lat(r):
        group = jnp.where((r == 0) & (pair < POLAR), ROUNDS, r) if plan.sparse else r

        def start(k, carry):
            peer = lax.rem(me + k, LATS)
            pltpu.make_async_remote_copy(
                src_ref=sent.at[r, peer],
                dst_ref=got.at[r, me],
                send_sem=lat_send.at[r],
                recv_sem=lat_recv.at[group],
                device_id=(peer, lev),
                device_id_type=MESH,
            ).start()
            return carry

        lax.fori_loop(1, LATS, start, 0)

    def send_lev(source, place, send, recv):
        def start(k, carry):
            peer = lax.rem(lev + k, LEVS)
            pltpu.make_async_remote_copy(
                src_ref=source.at[peer],
                dst_ref=place.at[lev],
                send_sem=send,
                recv_sem=recv,
                device_id=(me, peer),
                device_id_type=MESH,
            ).start()
            return carry

        lax.fori_loop(1, LEVS, start, 0)

    def turn(chunk):
        r, low, high = plan.chunks[chunk]
        first, last = plan.sources(chunk)
        group = ROUNDS if plan.sparse and chunk == 0 else r
        mine = (pair >= first) & (pair < last)
        messages = 2 * (last - first)

        @pl.when(mine)
        def _():
            await_bytes(got.at[r, pl.ds(0, messages - 1)], lat_recv.at[group])
            got[r, me] = sent[r, me]

        if messages < LATS:

            @pl.when(jnp.logical_not(mine))
            def _():
                await_bytes(got.at[r, pl.ds(0, messages)], lat_recv.at[group])

        for i in plan.pairs(chunk):
            north = got[r, i].astype(F32)
            south = got[r, LATS - 1 - i].astype(F32)
            folded[0, pl.ds(i * ROWS, ROWS), :] = north[:ROWS] + south[:ROWS]
            folded[1, pl.ds(i * ROWS, ROWS), :] = north[:ROWS] - south[:ROWS]
            if r == 0:
                flag_ref[...] = jnp.maximum(flag_ref[...], jnp.maximum(north[ROWS:], south[ROWS:]))
        row = iota((128, 128), 0)
        col = iota((128, 128), 1)
        source = 16 * (((row & 7) + me) & 7) + 8 * ((row >> 3) & 1) + (row >> 4)
        pick = one_hot(col == source)
        for part in range(2):
            values = dot_nt(pick, folded[part, low:high].astype(BF16)).astype(BF16)
            turned[chunk][part] = values.reshape(LEVS, 16, high - low)
            send_lev(turned[chunk].at[part], ready[chunk].at[part], lev_send.at[chunk, part], lev_recv.at[chunk, part])
        if plan.sparse and r:
            for part in range(2):
                values = dot_nt(pick, folded[part, low - 128 : low].astype(BF16))
                block = 2 * (r - 1) + part
                values = pltpu.roll(values, (EDGE * block + EDGE) % 128, 1)
                edges[...] = jnp.where((col >> 4) == block, values, edges[...])
            if r == 1:
                edge_sent[...] = edges[...].astype(BF16).reshape(LEVS, 16, 128)
                send_lev(edge_sent, edge_got, edge_send, edge_recv)

    def vertical_operator():
        pick_out = one_hot(iota((128, 64), 1) == (iota((128, 64), 0) >> 1))
        col = iota((64, 128), 1)
        pick_in = one_hot(iota((64, 128), 0) == 8 * (col >> 4) + (col & 7))
        same = (iota((128, 128), 0) & 1) == ((iota((128, 128), 1) >> 3) & 1)
        whole = vertical_ref[...]
        high = whole.astype(BF16)
        low = (whole - high.astype(F32)).astype(BF16)
        for k, term in enumerate((high, low)):
            term = dot_nt(pick_out, term).astype(BF16)
            term = dot(term, pick_in)
            mix[:, pl.ds(128 * k, 128)] = jnp.where(same, term, 0.0).astype(BF16)

    def mixed(values):
        values = values.reshape(128, values.shape[-1])
        return dot(mix[...], jnp.concatenate([values, values], axis=0))

    def received(chunk, part):
        await_bytes(ready[chunk].at[part, pl.ds(0, LEVS - 1)], lev_recv.at[chunk, part])
        ready[chunk][part, lev] = turned[chunk][part, lev]
        return mixed(ready[chunk][part]).astype(BF16)

    def legendre(r, edge):
        width = HALF - 128 * r
        wave = wave_ref[(me * LEVS + lev) * ROUNDS + r]
        for part in range(2):
            pieces = [received(k, part) for k in range(count) if plan.chunks[k][0] == r]
            if edge is not None and r:
                block = 2 * (r - 1) + part
                piece = pltpu.roll(edge, (128 - EDGE - EDGE * block) % 128, 1)
                pieces.insert(0, jnp.where(iota((128, 128), 1) >= 128 - EDGE, piece, 0.0).astype(BF16))
            values = jnp.concatenate(pieces, axis=1) if len(pieces) > 1 else pieces[0]
            table_copies[r, part].wait()
            start = plan.table_start(r)
            total = dot(values, table[r, start:, pl.ds(part * HALF, width)])
            degree = wave + 2 * iota((128, width), 1) + part
            total = jnp.where(degree < NT, total, 0.0)
            result[r, :, :, pl.ds(part * HALF, width)] = total.reshape(64, 2, width)
            if width < HALF:
                result[r, :, :, pl.ds(part * HALF + width, HALF - width)] = jnp.zeros((64, 2, HALF - width), F32)
        pltpu.make_async_copy(result.at[r], out_ref.at[:, r], out_sem.at[r]).start()

    grid_copy.wait()

    def advance(step, carry):
        r, due = round_at(step)

        @pl.when(due)
        def _():
            basis_copy(r).wait()
            fourier(r)

        @pl.when(step == 0)
        def _():
            pl.semaphore_wait(barrier, LATS - 1 + LEVS - 1)

        @pl.when(due)
        def _():
            send_lat(r)

        @pl.when(step == 0)
        def _():
            vertical_operator()

        for chunk in range(count):

            @pl.when(step == plan.turn_step[chunk])
            def _():
                turn(chunk)

        return carry

    lax.fori_loop(0, ROUNDS + 1, advance, 0)
    edge = None
    if plan.sparse:
        await_bytes(edge_got.at[pl.ds(0, LEVS - 1)], edge_recv)
        edge_got[lev] = edge_sent[lev]
        edge = mixed(edge_got[...])
    for r in reversed(range(ROUNDS)):
        legendre(r, edge)
    for r in range(ROUNDS):
        pltpu.make_async_copy(result.at[r], out_ref.at[:, r], out_sem.at[r]).wait()

    def drain_lat(r, carry):
        @pl.when(sends(r))
        def _():
            await_bytes(sent.at[r, pl.ds(0, LATS - 1)], lat_send.at[r])

        return carry

    lax.fori_loop(0, ROUNDS, drain_lat, 0)
    for chunk in range(count):
        for part in range(2):
            await_bytes(turned[chunk].at[part, pl.ds(0, LEVS - 1)], lev_send.at[chunk, part])
    if plan.sparse:
        await_bytes(edge_sent.at[pl.ds(0, LEVS - 1)], edge_send)


def transform(plan, collective_id, wave_table, wave_row, lon_count, vertical, grid_field, basis, legendre):
    anywhere = pl.BlockSpec(memory_space=pl.ANY)
    vmem = pl.BlockSpec(memory_space=pltpu.VMEM)
    smem = pl.BlockSpec(memory_space=pltpu.SMEM)
    count = len(plan.chunks)
    chunk_shapes = [pltpu.VMEM((2, LEVS, 16, high - low), BF16) for _, low, high in plan.chunks]
    return pl.pallas_call(
        functools.partial(kernel, plan),
        out_shape=[
            jax.ShapeDtypeStruct((64, ROUNDS, 2, NT), F32),
            jax.ShapeDtypeStruct((PAD - ROWS, 128), F32),
        ],
        in_specs=[smem, smem, vmem, vmem, anywhere, anywhere, anywhere],
        out_specs=[anywhere, vmem],
        scratch_shapes=[
            pltpu.VMEM((ROWS, NV, NLON), BF16),
            pltpu.VMEM((ROUNDS, NLON // 2, 2 * WAVES), BF16),
            pltpu.VMEM((ROUNDS, HALF, NT), BF16),
            pltpu.VMEM((ROWS * NV, 128), jnp.int32),
            pltpu.VMEM((2 * WAVES, 2 * WAVES), BF16),
            pltpu.VMEM((NV * PAD, ROWS * NV), BF16),
            pltpu.VMEM((128, 256), BF16),
            pltpu.VMEM((2, HALF, 128), F32),
            pltpu.VMEM((128, 128), F32),
            pltpu.VMEM((ROUNDS, LATS, PAD, 128), BF16),
            pltpu.VMEM((ROUNDS, LATS, PAD, 128), BF16),
            pltpu.VMEM((LEVS, 16, 128), BF16),
            pltpu.VMEM((LEVS, 16, 128), BF16),
            pltpu.VMEM((ROUNDS, 64, 2, NT), F32),
            *chunk_shapes,
            *chunk_shapes,
            pltpu.SemaphoreType.DMA,
            pltpu.SemaphoreType.DMA((ROUNDS,)),
            pltpu.SemaphoreType.DMA((ROUNDS, 2)),
            pltpu.SemaphoreType.DMA((ROUNDS,)),
            pltpu.SemaphoreType.DMA((ROUNDS,)),
            pltpu.SemaphoreType.DMA((ROUNDS + 1,)),
            pltpu.SemaphoreType.DMA((count, 2)),
            pltpu.SemaphoreType.DMA((count, 2)),
            pltpu.SemaphoreType.DMA,
            pltpu.SemaphoreType.DMA,
        ],
        compiler_params=pltpu.CompilerParams(
            collective_id=collective_id, has_side_effects=True, vmem_limit_bytes=56 << 20
        ),
        cost_estimate=pl.CostEstimate(flops=6_000_000_000, bytes_accessed=24_000_000, transcendentals=0),
    )(wave_table, lon_count, wave_row, vertical, grid_field, basis, legendre)


def on_device(grid_field, lon_count, wave_table, legendre, vertical):
    basis = jnp.asarray(basis_constant())
    args = (wave_table, wave_table.reshape(1, NT), lon_count, vertical, grid_field, basis, legendre)
    spectral, flag = transform(Plan(True), 0, *args)
    spectral = lax.cond(
        flag[0, 0] > 0, lambda kept, *rest: transform(Plan(False), 1, *rest)[0], lambda kept, *rest: kept, spectral, *args
    )
    return spectral.transpose(0, 2, 1, 3)


def solution(mesh):
    return jax.shard_map(
        on_device,
        mesh=mesh,
        in_specs=(P("lat", "lev", None), P("lat"), P(), P(("lat", "lev"), None, None), P()),
        out_specs=P(None, None, ("lat", "lev"), None),
        check_vma=False,
    )
```

time: 73.9 us -> 55.7 us (0.75)
  the two profiles are of different devices: /device:TPU:7 before, /device:TPU:1 now
where the time goes in v2:
time: 55.7 us; the launch traced here: 55.5 us
  Pallas kernels  51 us (92%)
  local copies, waits for them, and re-layouts  3.62 us (6%)
  between operations  0.7 us (1%)
    pallas_call x1, Pallas kernels, transform(): pl.pallas_call(functools.partial(kernel, plan), out_shape=[jax.ShapeDtype...  51 us
    unnamed x7, local copies, waits for them, and re-layouts  1.72 us
    slice x1, local copies, waits for them, and re-layouts, on_device(): flag[0, 0] > 0  1.19 us

profile of v2, /device:TPU:1, one launch (start us, length us, event | category | flops | bytes accessed | tf_op | source)
XLA Modules:
  0.0 55.5 jit_solution(15415739088443618585)
XLA Ops:
  0.0 0.7 %reshape.7.refs_2_ = s32[1,1280]{1,0:T(1,128)S(1)} reshape(s32[1280]{0:T(1024)} %refs_0_.1) | data formatting | bytes 10240 | tf_op jit(solution)/shard_map/reshape | solution.py:432
  0.7 0.0 copy-start
  0.7 0.0 copy-start.1
  0.7 0.0 copy-start.2
  0.7 51.0 %shard_map.64 = (f32[64,5,2,1280]{3,2,1,0:T(2,128)S(1)}, f32[8,128]{1,0:T(8,128)}) custom-call(s32[1280]{0:T(1024)} %refs_0_.1, s32[40]{0:T(128)} %refs_1_.1, s32[1,1280]{1,0:T(1,128)S(1)} %reshape.7.refs_2_, f32[64,64]{1,0:T(8,128)} %refs_3_.1, bf16[40,8,2560]{2,1,0:T(8,128)(2,1)} %refs_4_.1, bf16[5,1280,512]{2,1,0:T(8,128)(2,1)} %constant.5.clone.refs_5_, ...), custom_call_target="tpu_custom_call" | custom-call | flops 6000000000 | bytes 24000000 | tf_op jit(solution)/shard_map/pallas_call | solution.py:387
  51.7 1.2 %slice.3 = f32[1,1]{1,0:T(1,128)} slice(f32[8,128]{1,0:T(8,128)} %get-tuple-element.33), slice={[0:1], [0:1]} | slice | bytes 8 | tf_op jit(solution)/shard_map/slice | solution.py:435
  53.6 0.0 copy-done
  53.6 0.0 copy-done.1
  53.6 0.0 copy-done.2
  53.6 0.2 conditional.1
  53.8 1.7 %copy.10 = f32[64,2,5,1280]{3,1,2,0:T(2,128)} copy(f32[64,2,5,1280]{3,1,2,0:T(2,128)S(1)} %bitcast.2) | data formatting | bytes 6553600
Async XLA Ops:
  0.7 52.9 %copy-start = (s32[1280]{0:T(1024)S(1)}, s32[1280]{0:T(1024)}, u32[]{:S(2)}) copy-start(s32[1280]{0:T(1024)} %refs_0_.1) | copy-start | bytes 15364
  0.7 52.9 %copy-start.1 = (f32[64,64]{1,0:T(8,128)S(1)}, f32[64,64]{1,0:T(8,128)}, u32[]{:S(2)}) copy-start(f32[64,64]{1,0:T(8,128)} %refs_3_.1) | copy-start | bytes 49156
  0.7 52.9 %copy-start.2 = (s32[40]{0:T(128)S(1)}, s32[40]{0:T(128)}, u32[]{:S(2)}) copy-start(s32[40]{0:T(128)} %refs_1_.1) | copy-start | bytes 484

commit v3 on v2

--- a/solution.py
+++ b/solution.py
@@ -25,6 +25,7 @@
 POLAR = 7
 F32 = jnp.float32
 BF16 = jnp.bfloat16
+PEERS = (16, 2, 8, 4, 24, 6, 1, 18, 10, 20, 26, 12, 28, 14, 30, 22, 17, 3, 9, 5, 25, 7, 19, 11, 21, 27, 13, 29, 15, 31, 23)
 
 
 class Plan:
@@ -32,12 +33,14 @@
         self.sparse = sparse
         if sparse:
             self.first_pair = [0] + [(128 * r - EDGE) // ROWS for r in range(1, ROUNDS)]
-            self.chunks = [(0, 0, 256), (4, 512, HALF), (3, 384, HALF), (2, 256, HALF), (1, 128, HALF), (0, 256, HALF)]
-            self.turn_step = [1, 1, 2, 3, 4, 5]
+            self.chunks = [(0, 0, 256), (3, 384, HALF), (2, 256, HALF), (1, 128, HALF), (0, 256, HALF), (4, 512, HALF)]
+            self.turn_step = [2, 2, 3, 4, 5, 6]
+            self.sums = (3, 2, 1, 0, 4)
         else:
             self.first_pair = [0] * ROUNDS
             self.chunks = [(r, 0, HALF) for r in range(ROUNDS)]
             self.turn_step = [r + 1 for r in range(ROUNDS)]
+            self.sums = tuple(range(ROUNDS))
 
     def pairs(self, chunk):
         r, low, high = self.chunks[chunk]
@@ -91,8 +94,8 @@
 def kernel(plan, *refs):
     (
         wave_ref, lon_ref, wave_row_ref, vertical_ref, grid_ref, basis_ref, legendre_ref,
-        out_ref, flag_ref,
-        x, basis, table, lon, route, order, mix, folded, edges, sent, got, edge_sent, edge_got, result, *chunk_refs,
+        out_ref, flag_out,
+        x, flag_ref, basis, table, lon, route, order, mix, folded, edges, sent, got, edge_sent, edge_got, result, *chunk_refs,
     ) = refs
     count = len(plan.chunks)
     turned, ready = chunk_refs[:count], chunk_refs[count : 2 * count]
@@ -112,11 +115,11 @@
     def round_at(step):
         if not plan.sparse:
             return step, step < ROUNDS
-        usual = ROUNDS - 1 - step
+        usual = jnp.where(step == ROUNDS - 1, ROUNDS - 1, ROUNDS - 2 - step)
         early = (pair < POLAR) & (step == 0)
         r = jnp.where(early, 0, usual)
         due = early | ((step > 0) | (pair >= POLAR)) & sends(usual) & ~((pair < POLAR) & (usual == 0))
-        return jnp.maximum(r, 0), due & (usual >= 0)
+        return jnp.maximum(r, 0), due & (step < ROUNDS)
 
     def basis_copy(r):
         return pltpu.make_async_copy(basis_ref.at[r], basis.at[r], basis_sem.at[r])
@@ -161,7 +164,7 @@
     row = iota((NT, 2 * WAVES), 0)
     col = iota((NT, 2 * WAVES), 1)
     pick = one_hot(row == ROUNDS * (8 * (col >> 4) + (col & 7)))
-    waves = jnp.broadcast_to(wave_row_ref[...].astype(F32), (8, NT)).astype(BF16)
+    waves = jnp.broadcast_to(wave_row_ref[...].reshape(1, NT).astype(F32), (8, NT)).astype(BF16)
     place = dot(waves, pick).astype(jnp.int32)
     target = WAVES * (place & 1) + 128 * ((iota((8, 2 * WAVES), 1) >> 3) & 1) + (place >> 1)
     route[...] = one_hot(iota((2 * WAVES, 2 * WAVES), 0) == target[:1])
@@ -208,8 +211,8 @@
     def send_lat(r):
         group = jnp.where((r == 0) & (pair < POLAR), ROUNDS, r) if plan.sparse else r
 
-        def start(k, carry):
-            peer = lax.rem(me + k, LATS)
+        for k in PEERS:
+            peer = me ^ k
             pltpu.make_async_remote_copy(
                 src_ref=sent.at[r, peer],
                 dst_ref=got.at[r, me],
@@ -218,13 +221,10 @@
                 device_id=(peer, lev),
                 device_id_type=MESH,
             ).start()
-            return carry
-
-        lax.fori_loop(1, LATS, start, 0)
 
     def send_lev(source, place, send, recv):
-        def start(k, carry):
-            peer = lax.rem(lev + k, LEVS)
+        for k in (4, 3, 5, 2, 6, 1, 7):
+            peer = (lev + k) & (LEVS - 1)
             pltpu.make_async_remote_copy(
                 src_ref=source.at[peer],
                 dst_ref=place.at[lev],
@@ -233,9 +233,9 @@
                 device_id=(me, peer),
                 device_id_type=MESH,
             ).start()
-            return carry
-
-        lax.fori_loop(1, LEVS, start, 0)
+
+    def edge_place(r, part):
+        return (1, part) if r == 4 else (0, 2 * (r - 1) + part)
 
     def turn(chunk):
         r, low, high = plan.chunks[chunk]
@@ -273,12 +273,12 @@
         if plan.sparse and r:
             for part in range(2):
                 values = dot_nt(pick, folded[part, low - 128 : low].astype(BF16))
-                block = 2 * (r - 1) + part
+                tile, block = edge_place(r, part)
                 values = pltpu.roll(values, (EDGE * block + EDGE) % 128, 1)
-                edges[...] = jnp.where((col >> 4) == block, values, edges[...])
-            if r == 1:
-                edge_sent[...] = edges[...].astype(BF16).reshape(LEVS, 16, 128)
-                send_lev(edge_sent, edge_got, edge_send, edge_recv)
+                edges[tile] = jnp.where((col >> 4) == block, values, edges[tile])
+            if r in (1, 4):
+                edge_sent[tile] = edges[tile].astype(BF16).reshape(LEVS, 16, 128)
+                send_lev(edge_sent.at[tile], edge_got.at[tile], edge_send.at[tile], edge_recv.at[tile])
 
     def vertical_operator():
         pick_out = one_hot(iota((128, 64), 1) == (iota((128, 64), 0) >> 1))
@@ -302,15 +302,24 @@
         ready[chunk][part, lev] = turned[chunk][part, lev]
         return mixed(ready[chunk][part]).astype(BF16)
 
-    def legendre(r, edge):
+    edge_values = {}
+
+    def edge_piece(r, part):
+        tile, block = edge_place(r, part)
+        if tile not in edge_values:
+            await_bytes(edge_got.at[tile, pl.ds(0, LEVS - 1)], edge_recv.at[tile])
+            edge_got[tile, lev] = edge_sent[tile, lev]
+            edge_values[tile] = mixed(edge_got[tile])
+        piece = pltpu.roll(edge_values[tile], (128 - EDGE - EDGE * block) % 128, 1)
+        return jnp.where(iota((128, 128), 1) >= 128 - EDGE, piece, 0.0).astype(BF16)
+
+    def legendre(r):
         width = HALF - 128 * r
         wave = wave_ref[(me * LEVS + lev) * ROUNDS + r]
         for part in range(2):
             pieces = [received(k, part) for k in range(count) if plan.chunks[k][0] == r]
-            if edge is not None and r:
-                block = 2 * (r - 1) + part
-                piece = pltpu.roll(edge, (128 - EDGE - EDGE * block) % 128, 1)
-                pieces.insert(0, jnp.where(iota((128, 128), 1) >= 128 - EDGE, piece, 0.0).astype(BF16))
+            if plan.sparse and r:
+                pieces.insert(0, edge_piece(r, part))
             values = jnp.concatenate(pieces, axis=1) if len(pieces) > 1 else pieces[0]
             table_copies[r, part].wait()
             start = plan.table_start(r)
@@ -352,14 +361,10 @@
 
         return carry
 
-    lax.fori_loop(0, ROUNDS + 1, advance, 0)
-    edge = None
-    if plan.sparse:
-        await_bytes(edge_got.at[pl.ds(0, LEVS - 1)], edge_recv)
-        edge_got[lev] = edge_sent[lev]
-        edge = mixed(edge_got[...])
-    for r in reversed(range(ROUNDS)):
-        legendre(r, edge)
+    lax.fori_loop(0, max(plan.turn_step) + 1, advance, 0)
+    flag_out[0] = (jnp.max(flag_ref[...]) > 0).astype(jnp.int32)
+    for r in plan.sums:
+        legendre(r)
     for r in range(ROUNDS):
         pltpu.make_async_copy(result.at[r], out_ref.at[:, r], out_sem.at[r]).wait()
 
@@ -375,7 +380,8 @@
         for part in range(2):
             await_bytes(turned[chunk].at[part, pl.ds(0, LEVS - 1)], lev_send.at[chunk, part])
     if plan.sparse:
-        await_bytes(edge_sent.at[pl.ds(0, LEVS - 1)], edge_send)
+        for tile in range(2):
+            await_bytes(edge_sent.at[tile, pl.ds(0, LEVS - 1)], edge_send.at[tile])
 
 
 def transform(plan, collective_id, wave_table, wave_row, lon_count, vertical, grid_field, basis, legendre):
@@ -388,12 +394,13 @@
         functools.partial(kernel, plan),
         out_shape=[
             jax.ShapeDtypeStruct((64, ROUNDS, 2, NT), F32),
-            jax.ShapeDtypeStruct((PAD - ROWS, 128), F32),
+            jax.ShapeDtypeStruct((1,), jnp.int32),
         ],
         in_specs=[smem, smem, vmem, vmem, anywhere, anywhere, anywhere],
-        out_specs=[anywhere, vmem],
+        out_specs=[anywhere, smem],
         scratch_shapes=[
             pltpu.VMEM((ROWS, NV, NLON), BF16),
+            pltpu.VMEM((PAD - ROWS, 128), F32),
             pltpu.VMEM((ROUNDS, NLON // 2, 2 * WAVES), BF16),
             pltpu.VMEM((ROUNDS, HALF, NT), BF16),
             pltpu.VMEM((ROWS * NV, 128), jnp.int32),
@@ -401,11 +408,11 @@
             pltpu.VMEM((NV * PAD, ROWS * NV), BF16),
             pltpu.VMEM((128, 256), BF16),
             pltpu.VMEM((2, HALF, 128), F32),
-            pltpu.VMEM((128, 128), F32),
+            pltpu.VMEM((2, 128, 128), F32),
             pltpu.VMEM((ROUNDS, LATS, PAD, 128), BF16),
             pltpu.VMEM((ROUNDS, LATS, PAD, 128), BF16),
-            pltpu.VMEM((LEVS, 16, 128), BF16),
-            pltpu.VMEM((LEVS, 16, 128), BF16),
+            pltpu.VMEM((2, LEVS, 16, 128), BF16),
+            pltpu.VMEM((2, LEVS, 16, 128), BF16),
             pltpu.VMEM((ROUNDS, 64, 2, NT), F32),
             *chunk_shapes,
             *chunk_shapes,
@@ -417,8 +424,8 @@
             pltpu.SemaphoreType.DMA((ROUNDS + 1,)),
             pltpu.SemaphoreType.DMA((count, 2)),
             pltpu.SemaphoreType.DMA((count, 2)),
-            pltpu.SemaphoreType.DMA,
-            pltpu.SemaphoreType.DMA,
+            pltpu.SemaphoreType.DMA((2,)),
+            pltpu.SemaphoreType.DMA((2,)),
         ],
         compiler_params=pltpu.CompilerParams(
             collective_id=collective_id, has_side_effects=True, vmem_limit_bytes=56 << 20
@@ -429,10 +436,10 @@
 
 def on_device(grid_field, lon_count, wave_table, legendre, vertical):
     basis = jnp.asarray(basis_constant())
-    args = (wave_table, wave_table.reshape(1, NT), lon_count, vertical, grid_field, basis, legendre)
+    args = (wave_table, wave_table, lon_count, vertical, grid_field, basis, legendre)
     spectral, flag = transform(Plan(True), 0, *args)
     spectral = lax.cond(
-        flag[0, 0] > 0, lambda kept, *rest: transform(Plan(False), 1, *rest)[0], lambda kept, *rest: kept, spectral, *args
+        flag[0] > 0, lambda kept, *rest: transform(Plan(False), 1, *rest)[0], lambda kept, *rest: kept, spectral, *args
     )
     return spectral.transpose(0, 2, 1, 3)
 

time: 55.7 us -> 49.2 us (0.88)
  Pallas kernels: 51 us -> 46.4 us
  local copies, waits for them, and re-layouts: 3.62 us -> 1.72 us
    pallas_call x1, Pallas kernels: 51 us -> 46.4 us  [transform(): pl.pallas_call(functools.partial(kernel, plan), out_shape=[jax.ShapeDtype...]
    slice x1 -> x0, local copies, waits for them, and re-layouts: 1.19 us -> none  [on_device(): flag[0, 0] > 0]
    reshape x1 -> x0, local copies, waits for them, and re-layouts: 0.7 us -> none  [on_device(): wave_table.reshape(1, NT)]
where the time goes in v3:
time: 49.2 us; the launch traced here: 49 us
  Pallas kernels  46.4 us (94%)
  local copies, waits for them, and re-layouts  1.72 us (3%)
  between operations  0.74 us (2%)
    pallas_call x1, Pallas kernels, transform(): pl.pallas_call(functools.partial(kernel, plan), out_shape=[jax.ShapeDtype...  46.4 us
    unnamed x7, local copies, waits for them, and re-layouts  1.72 us

profile of v3, /device:TPU:1, one launch (start us, length us, event | category | flops | bytes accessed | tf_op | source)
XLA Modules:
  0.0 49.0 jit_solution(5242302816832186404)
XLA Ops:
  0.0 0.0 copy-start
  0.0 0.0 copy-start.1
  0.0 0.0 copy-start.2
  0.0 46.4 %shard_map.64 = (f32[64,5,2,1280]{3,2,1,0:T(2,128)S(1)}, s32[1]{0:T(128)}) custom-call(s32[1280]{0:T(1024)} %refs_2_.1, s32[40]{0:T(128)} %refs_1_.1, s32[1280]{0:T(1024)} %refs_2_.1, f32[64,64]{1,0:T(8,128)} %refs_3_.1, bf16[40,8,2560]{2,1,0:T(8,128)(2,1)} %refs_4_.1, bf16[5,1280,512]{2,1,0:T(8,128)(2,1)} %constant.5.clone.refs_5_, ...), custom_call_target="tpu_custom_call" | custom-call | flops 6000000000 | bytes 24000000 | tf_op jit(solution)/shard_map/pallas_call | solution.py:393
  47.1 0.0 copy-done
  47.1 0.0 copy-done.1
  47.1 0.0 copy-done.2
  47.1 0.2 conditional.1
  47.3 1.7 %copy.10 = f32[64,2,5,1280]{3,1,2,0:T(2,128)} copy(f32[64,2,5,1280]{3,1,2,0:T(2,128)S(1)} %bitcast.2) | data formatting | bytes 6553600
Async XLA Ops:
  0.0 47.1 %copy-start = (f32[64,64]{1,0:T(8,128)S(1)}, f32[64,64]{1,0:T(8,128)}, u32[]{:S(2)}) copy-start(f32[64,64]{1,0:T(8,128)} %refs_3_.1) | copy-start | bytes 49156
  0.0 47.1 %copy-start.1 = (s32[1280]{0:T(1024)S(1)}, s32[1280]{0:T(1024)}, u32[]{:S(2)}) copy-start(s32[1280]{0:T(1024)} %refs_2_.1) | copy-start | bytes 15364
  0.0 47.1 %copy-start.2 = (s32[40]{0:T(128)S(1)}, s32[40]{0:T(128)}, u32[]{:S(2)}) copy-start(s32[40]{0:T(128)} %refs_1_.1) | copy-start | bytes 484

commit v4 on v3

--- a/solution.py
+++ b/solution.py
@@ -25,7 +25,7 @@
 POLAR = 7
 F32 = jnp.float32
 BF16 = jnp.bfloat16
-PEERS = (16, 2, 8, 4, 24, 6, 1, 18, 10, 20, 26, 12, 28, 14, 30, 22, 17, 3, 9, 5, 25, 7, 19, 11, 21, 27, 13, 29, 15, 31, 23)
+PEERS = (29, 18, 12, 11, 27, 2, 6, 31, 8, 17, 10, 20, 30, 14, 22, 1, 21, 24, 7, 13, 23, 15, 16, 4, 9, 3, 25, 26, 28, 19, 5)
 
 
 class Plan:
@@ -34,7 +34,7 @@
         if sparse:
             self.first_pair = [0] + [(128 * r - EDGE) // ROWS for r in range(1, ROUNDS)]
             self.chunks = [(0, 0, 256), (3, 384, HALF), (2, 256, HALF), (1, 128, HALF), (0, 256, HALF), (4, 512, HALF)]
-            self.turn_step = [2, 2, 3, 4, 5, 6]
+            self.turn_step = [3, 3, 4, 5, 6, 7]
             self.sums = (3, 2, 1, 0, 4)
         else:
             self.first_pair = [0] * ROUNDS
@@ -268,8 +268,8 @@
         pick = one_hot(col == source)
         for part in range(2):
             values = dot_nt(pick, folded[part, low:high].astype(BF16)).astype(BF16)
-            turned[chunk][part] = values.reshape(LEVS, 16, high - low)
-            send_lev(turned[chunk].at[part], ready[chunk].at[part], lev_send.at[chunk, part], lev_recv.at[chunk, part])
+            turned[chunk][:, part] = values.reshape(LEVS, 16, high - low)
+        send_lev(turned[chunk], ready[chunk], lev_send.at[chunk], lev_recv.at[chunk])
         if plan.sparse and r:
             for part in range(2):
                 values = dot_nt(pick, folded[part, low - 128 : low].astype(BF16))
@@ -298,9 +298,10 @@
         return dot(mix[...], jnp.concatenate([values, values], axis=0))
 
     def received(chunk, part):
-        await_bytes(ready[chunk].at[part, pl.ds(0, LEVS - 1)], lev_recv.at[chunk, part])
-        ready[chunk][part, lev] = turned[chunk][part, lev]
-        return mixed(ready[chunk][part]).astype(BF16)
+        if part == 0:
+            await_bytes(ready[chunk].at[pl.ds(0, LEVS - 1)], lev_recv.at[chunk])
+            ready[chunk][lev] = turned[chunk][lev]
+        return mixed(ready[chunk][:, part]).astype(BF16)
 
     edge_values = {}
 
@@ -377,8 +378,7 @@
 
     lax.fori_loop(0, ROUNDS, drain_lat, 0)
     for chunk in range(count):
-        for part in range(2):
-            await_bytes(turned[chunk].at[part, pl.ds(0, LEVS - 1)], lev_send.at[chunk, part])
+        await_bytes(turned[chunk].at[pl.ds(0, LEVS - 1)], lev_send.at[chunk])
     if plan.sparse:
         for tile in range(2):
             await_bytes(edge_sent.at[tile, pl.ds(0, LEVS - 1)], edge_send.at[tile])
@@ -389,7 +389,7 @@
     vmem = pl.BlockSpec(memory_space=pltpu.VMEM)
     smem = pl.BlockSpec(memory_space=pltpu.SMEM)
     count = len(plan.chunks)
-    chunk_shapes = [pltpu.VMEM((2, LEVS, 16, high - low), BF16) for _, low, high in plan.chunks]
+    chunk_shapes = [pltpu.VMEM((LEVS, 2, 16, high - low), BF16) for _, low, high in plan.chunks]
     return pl.pallas_call(
         functools.partial(kernel, plan),
         out_shape=[
@@ -422,8 +422,8 @@
             pltpu.SemaphoreType.DMA((ROUNDS,)),
             pltpu.SemaphoreType.DMA((ROUNDS,)),
             pltpu.SemaphoreType.DMA((ROUNDS + 1,)),
-            pltpu.SemaphoreType.DMA((count, 2)),
-            pltpu.SemaphoreType.DMA((count, 2)),
+            pltpu.SemaphoreType.DMA((count,)),
+            pltpu.SemaphoreType.DMA((count,)),
             pltpu.SemaphoreType.DMA((2,)),
             pltpu.SemaphoreType.DMA((2,)),
         ],

time: 49.2 us -> 48.5 us (0.986)
  Pallas kernels: 46.4 us -> 45.7 us
    pallas_call x1, Pallas kernels: 46.4 us -> 45.7 us  [transform(): pl.pallas_call(functools.partial(kernel, plan), out_shape=[jax.ShapeDtype...]
where the time goes in v4:
time: 48.5 us; the launch traced here: 48.3 us
  Pallas kernels  45.7 us (94%)
  local copies, waits for them, and re-layouts  1.72 us (4%)
  between operations  0.74 us (2%)
    pallas_call x1, Pallas kernels, transform(): pl.pallas_call(functools.partial(kernel, plan), out_shape=[jax.ShapeDtype...  45.7 us
    unnamed x7, local copies, waits for them, and re-layouts  1.72 us

profile of v4, /device:TPU:1, one launch (start us, length us, event | category | flops | bytes accessed | tf_op | source)
XLA Modules:
  0.0 48.3 jit_solution(3619756968230773013)
XLA Ops:
  0.0 0.0 copy-start
  0.0 0.0 copy-start.1
  0.0 0.0 copy-start.2
  0.0 45.7 %shard_map.64 = (f32[64,5,2,1280]{3,2,1,0:T(2,128)S(1)}, s32[1]{0:T(128)}) custom-call(s32[1280]{0:T(1024)} %refs_2_.1, s32[40]{0:T(128)} %refs_1_.1, s32[1280]{0:T(1024)} %refs_2_.1, f32[64,64]{1,0:T(8,128)} %refs_3_.1, bf16[40,8,2560]{2,1,0:T(8,128)(2,1)} %refs_4_.1, bf16[5,1280,512]{2,1,0:T(8,128)(2,1)} %constant.5.clone.refs_5_, ...), custom_call_target="tpu_custom_call" | custom-call | flops 6000000000 | bytes 24000000 | tf_op jit(solution)/shard_map/pallas_call | solution.py:393
  46.4 0.0 copy-done
  46.4 0.0 copy-done.1
  46.4 0.0 copy-done.2
  46.4 0.2 conditional.1
  46.6 1.7 %copy.10 = f32[64,2,5,1280]{3,1,2,0:T(2,128)} copy(f32[64,2,5,1280]{3,1,2,0:T(2,128)S(1)} %bitcast.2) | data formatting | bytes 6553600
Async XLA Ops:
  0.0 46.4 %copy-start = (f32[64,64]{1,0:T(8,128)S(1)}, f32[64,64]{1,0:T(8,128)}, u32[]{:S(2)}) copy-start(f32[64,64]{1,0:T(8,128)} %refs_3_.1) | copy-start | bytes 49156
  0.0 46.4 %copy-start.1 = (s32[1280]{0:T(1024)S(1)}, s32[1280]{0:T(1024)}, u32[]{:S(2)}) copy-start(s32[1280]{0:T(1024)} %refs_2_.1) | copy-start | bytes 15364
  0.0 46.4 %copy-start.2 = (s32[40]{0:T(128)S(1)}, s32[40]{0:T(128)}, u32[]{:S(2)}) copy-start(s32[40]{0:T(128)} %refs_1_.1) | copy-start | bytes 484
